TPU v7x, 32 devices: a whole 2x2x4 slice. The times are simulated.
32 devices in a mesh: gx: 8 (over z, x), gy: 4 (over y, core).
Axes of the slice: x: 2, y: 2, z: 4, core: 2. Of those that a mesh axis runs over, the one named last changes fastest.
Arguments:
- tokens: bfloat16 [256, 128, 768], P(('gx', 'gy')), may hold values from -6 to 6
- land_mask: int32 [256, 128], P(('gx', 'gy')), may hold values from 0 to 1, as said below
- counts: int32 [256], replicated, may hold values from 1 to 128, as said below
- ln1_gain: bfloat16 [768], P(('gx', 'gy')), may hold values from 0.099609375 to 1.8984375
- ln1_shift: bfloat16 [768], P(('gx', 'gy')), may hold values from -3 to 3
- qkv_weight: bfloat16 [768, 2304], P(('gx', 'gy')), may hold values from -0.21875 to 0.21875
- qv_bias: bfloat16 [2, 768], P(None, ('gx', 'gy')), may hold values from -3 to 3
- out_weight: bfloat16 [768, 768], P(('gx', 'gy')), may hold values from -0.875 to 0.875
- out_bias: bfloat16 [768], P(('gx', 'gy')), may hold values from -3 to 3
- ln2_gain: bfloat16 [768], P(('gx', 'gy')), may hold values from 0.099609375 to 1.8984375
- ln2_shift: bfloat16 [768], P(('gx', 'gy')), may hold values from -3 to 3
- up_weight: bfloat16 [768, 3072], P(('gx', 'gy')), may hold values from -0.21875 to 0.21875
- up_bias: bfloat16 [3072], P(('gx', 'gy')), may hold values from -3 to 3
- down_weight: bfloat16 [3072, 768], P(('gx', 'gy')), may hold values from -0.109375 to 0.109375
- down_bias: bfloat16 [768], P(('gx', 'gy')), may hold values from -3 to 3
- cotangent: bfloat16 [256, 128, 768], P(('gx', 'gy')), may hold values from -6 to 6
Outputs:
- out_tokens: bfloat16 [256, 128, 768], P(('gx', 'gy'))
- grad_tokens: bfloat16 [256, 128, 768], P(('gx', 'gy'))
- grad_ln1_gain: float32 [768], P(('gx', 'gy'))
- grad_ln1_shift: float32 [768], P(('gx', 'gy'))
- grad_qkv_weight: float32 [768, 2304], P(('gx', 'gy'))
- grad_qv_bias: float32 [2, 768], P(None, ('gx', 'gy'))
- grad_out_weight: float32 [768, 768], P(('gx', 'gy'))
- grad_out_bias: float32 [768], P(('gx', 'gy'))
- grad_ln2_gain: float32 [768], P(('gx', 'gy'))
- grad_ln2_shift: float32 [768], P(('gx', 'gy'))
- grad_up_weight: float32 [768, 3072], P(('gx', 'gy'))
- grad_up_bias: float32 [3072], P(('gx', 'gy'))
- grad_down_weight: float32 [3072, 768], P(('gx', 'gy'))
- grad_down_bias: float32 [768], P(('gx', 'gy'))
Inputs may be any that keep to these rules, and one draw needn't show every extreme that they name: `land_mask`: each sample has at least as many land patches as its count. Sample i of a device (in the device's own order) is processed by the device with gy index i mod 4 and the same gx index. On every device, the counts of the samples that go to one gy index add up to at most 3 * 128 * 2 / 4 (192 here); exactly that for some pair of devices in every draw.
All inputs are finite; a program needn't handle non-finite values.
Results may differ from a plain program's by a relative error of at most 0.012.
Values may be sent and summed in bfloat16 or wider, within the bound.
A program may use at most 192 MiB of HBM per device.

v0:
```python
import math

import jax
import jax.numpy as jnp
from jax import lax
from jax.sharding import PartitionSpec as P

HEADS = 12
HD = 64


def layer_norm(values, gain, shift):
    center = values - jnp.mean(values, axis=-1, keepdims=True)
    spread = jnp.mean(center * center, axis=-1, keepdims=True)
    return center * lax.rsqrt(spread + 1e-05) * gain + shift


def gelu_exact(values):
    return jax.nn.gelu(values, approximate=False)


def trans_dot(left, right):
    return lax.dot_general(
        left, right, (((0,), (0,)), ((), ())), preferred_element_type=jnp.float32
    )


def back_dot(left, right):
    return lax.dot_general(
        left, right, (((1,), (1,)), ((), ())), preferred_element_type=jnp.float32
    )


def start_rows(sample_counts, gy_count):
    grouped = sample_counts.reshape(sample_counts.shape[:-1] + (-1, gy_count))
    return (jnp.cumsum(grouped, axis=-2) - grouped).reshape(sample_counts.shape)


def attend_forward(pieces):
    query_rows, key_rows, value_rows, labels = pieces
    score_scale = query_rows.shape[-1] ** (-0.5)
    allowed = labels[:, :, None] == labels[:, None, :]
    scores = (
        jnp.einsum("gqhe,gkhe->ghqk", query_rows, key_rows, preferred_element_type=jnp.float32)
        * score_scale
    )
    scores = jnp.where(allowed[:, None], scores, -1000000000.0)
    row_peak = jnp.max(scores, axis=-1, keepdims=True)
    expo = jnp.exp(scores - row_peak)
    row_total = jnp.sum(expo, axis=-1, keepdims=True)
    attn_probs = (expo / row_total).astype(jnp.bfloat16)
    context = jnp.einsum(
        "ghqk,gkhe->gqhe", attn_probs, value_rows, preferred_element_type=jnp.float32
    )
    return (context.astype(jnp.bfloat16), row_peak[..., 0] + jnp.log(row_total[..., 0]))


def attend_backward(pieces):
    query_rows, key_rows, value_rows, labels, log_total, grad_context = pieces
    score_scale = query_rows.shape[-1] ** (-0.5)
    allowed = labels[:, :, None] == labels[:, None, :]
    scores = (
        jnp.einsum("gqhe,gkhe->ghqk", query_rows, key_rows, preferred_element_type=jnp.float32)
        * score_scale
    )
    scores = jnp.where(allowed[:, None], scores, -1000000000.0)
    probs_full = jnp.exp(scores - log_total[..., None])
    probs_low = probs_full.astype(jnp.bfloat16)
    grad_probs = jnp.einsum(
        "gqhe,gkhe->ghqk", grad_context, value_rows, preferred_element_type=jnp.float32
    )
    row_delta = jnp.sum(probs_full * grad_probs, axis=-1, keepdims=True)
    grad_scores = (probs_full * (grad_probs - row_delta)).astype(jnp.bfloat16)
    grad_query = (
        jnp.einsum("ghqk,gkhe->gqhe", grad_scores, key_rows, preferred_element_type=jnp.float32)
        * score_scale
    )
    grad_key = (
        jnp.einsum("ghqk,gqhe->gkhe", grad_scores, query_rows, preferred_element_type=jnp.float32)
        * score_scale
    )
    grad_value = jnp.einsum(
        "ghqk,gqhe->gkhe", probs_low, grad_context, preferred_element_type=jnp.float32
    )
    return (
        grad_query.astype(jnp.bfloat16),
        grad_key.astype(jnp.bfloat16),
        grad_value.astype(jnp.bfloat16),
    )


def per_device(
    tokens,
    land_mask,
    counts,
    ln1_gain,
    ln1_shift,
    qkv_weight,
    qv_bias,
    out_weight,
    out_bias,
    ln2_gain,
    ln2_shift,
    up_weight,
    up_bias,
    down_weight,
    down_bias,
    cotangent,
):
    gathered = (
        lax.all_gather(ln1_gain, ("gx", "gy"), axis=0, tiled=True),
        lax.all_gather(ln1_shift, ("gx", "gy"), axis=0, tiled=True),
        lax.all_gather(qkv_weight, ("gx", "gy"), axis=0, tiled=True),
        lax.all_gather(qv_bias, ("gx", "gy"), axis=1, tiled=True),
        lax.all_gather(out_weight, ("gx", "gy"), axis=0, tiled=True),
        lax.all_gather(out_bias, ("gx", "gy"), axis=0, tiled=True),
        lax.all_gather(ln2_gain, ("gx", "gy"), axis=0, tiled=True),
        lax.all_gather(ln2_shift, ("gx", "gy"), axis=0, tiled=True),
        lax.all_gather(up_weight, ("gx", "gy"), axis=0, tiled=True),
        lax.all_gather(up_bias, ("gx", "gy"), axis=0, tiled=True),
        lax.all_gather(down_weight, ("gx", "gy"), axis=0, tiled=True),
        lax.all_gather(down_bias, ("gx", "gy"), axis=0, tiled=True),
    )
    samples, patches, model_width = tokens.shape
    gy_count = lax.axis_size("gy")
    row_index = lax.axis_index("gy")
    column_index = lax.axis_index("gx")
    device = column_index * gy_count + row_index
    own_count = lax.dynamic_slice_in_dim(counts, device * samples, samples)
    land_rank = jnp.cumsum(land_mask, axis=1) - 1
    kept = (land_mask == 1) & (land_rank < own_count[:, None])
    visible = kept.reshape(-1)
    per_peer = samples // gy_count
    slot_capacity = 3 * patches * per_peer // 4
    own_dest = jnp.arange(samples, dtype=jnp.int32) % gy_count
    own_offset = start_rows(own_count, gy_count)
    target = own_dest[:, None] * slot_capacity + own_offset[:, None] + land_rank
    target = jnp.where(kept, target, gy_count * slot_capacity).reshape(-1)
    send_rows = (
        jnp.zeros((gy_count * slot_capacity, model_width), jnp.bfloat16)
        .at[target]
        .set(tokens.reshape(-1, model_width), mode="drop")
    )
    send_grads = (
        jnp.zeros((gy_count * slot_capacity, model_width), jnp.bfloat16)
        .at[target]
        .set(cotangent.reshape(-1, model_width), mode="drop")
    )
    arrived_rows, arrived_grads = (
        lax.all_to_all(
            send_rows.reshape(gy_count, slot_capacity, model_width),
            "gy",
            split_axis=0,
            concat_axis=0,
            tiled=True,
        ),
        lax.all_to_all(
            send_grads.reshape(gy_count, slot_capacity, model_width),
            "gy",
            split_axis=0,
            concat_axis=0,
            tiled=True,
        ),
    )
    team_start = column_index * gy_count * samples
    team_count = lax.dynamic_slice_in_dim(counts, team_start, gy_count * samples).reshape(
        gy_count, samples
    )
    team_offset = start_rows(team_count, gy_count)
    team_dest = jnp.broadcast_to(
        (jnp.arange(samples, dtype=jnp.int32) % gy_count)[None, :], (gy_count, samples)
    )
    slot_rows = jnp.arange(slot_capacity, dtype=jnp.int32)
    member = (
        (team_dest[:, :, None] == row_index)
        & (slot_rows[None, None, :] >= team_offset[:, :, None])
        & (slot_rows[None, None, :] < team_offset[:, :, None] + team_count[:, :, None])
    )
    label_ids = (
        jnp.arange(gy_count, dtype=jnp.int32)[:, None] * samples
        + jnp.arange(samples, dtype=jnp.int32)[None, :]
        + 1
    )
    labels = (jnp.sum(jnp.where(member, label_ids[:, :, None], 0), axis=1) - 1).reshape(-1)
    rows_in = arrived_rows.reshape(-1, model_width)
    rows_grad = arrived_grads.reshape(-1, model_width)
    per_step = math.gcd(gy_count, max(1, -(-512 // slot_capacity)))
    (
        gain_one,
        shift_one,
        qkv_full,
        bias_qv,
        out_full,
        bias_out,
        gain_two,
        shift_two,
        up_full,
        bias_up,
        down_full,
        bias_down,
    ) = gathered
    total_rows = rows_in.shape[0]
    inputs = rows_in.astype(jnp.float32)
    normed_f, norm_one_pull = jax.vjp(
        layer_norm, inputs, gain_one.astype(jnp.float32), shift_one.astype(jnp.float32)
    )
    normed = normed_f.astype(jnp.bfloat16)
    joined_qkv = jnp.dot(normed, qkv_full, preferred_element_type=jnp.float32)
    bias_pair = bias_qv.astype(jnp.float32)
    queries = (joined_qkv[:, :model_width] + bias_pair[0]).astype(jnp.bfloat16)
    key_rows = joined_qkv[:, model_width : 2 * model_width].astype(jnp.bfloat16)
    value_rows = (joined_qkv[:, 2 * model_width :] + bias_pair[1]).astype(jnp.bfloat16)
    step_count = gy_count // per_step
    head_shape = (step_count, per_step, slot_capacity, HEADS, HD)
    query_blocks = queries.reshape(head_shape)
    key_blocks = key_rows.reshape(head_shape)
    value_blocks = value_rows.reshape(head_shape)
    label_blocks = labels.reshape(step_count, per_step, slot_capacity)
    context_blocks, log_totals = lax.map(
        attend_forward, (query_blocks, key_blocks, value_blocks, label_blocks)
    )
    context = context_blocks.reshape(total_rows, model_width)
    middle = (
        inputs
        + jnp.dot(context, out_full, preferred_element_type=jnp.float32)
        + bias_out.astype(jnp.float32)
    )
    normed_two_f, norm_two_pull = jax.vjp(
        layer_norm, middle, gain_two.astype(jnp.float32), shift_two.astype(jnp.float32)
    )
    normed_two = normed_two_f.astype(jnp.bfloat16)
    hidden = jnp.dot(normed_two, up_full, preferred_element_type=jnp.float32) + bias_up.astype(
        jnp.float32
    )
    active_f, gelu_pull = jax.vjp(gelu_exact, hidden)
    active = active_f.astype(jnp.bfloat16)
    result = (
        middle
        + jnp.dot(active, down_full, preferred_element_type=jnp.float32)
        + bias_down.astype(jnp.float32)
    )
    output_rows = result.astype(jnp.bfloat16)
    refetch = (
        lax.all_gather(ln1_gain, ("gx", "gy"), axis=0, tiled=True),
        lax.all_gather(ln1_shift, ("gx", "gy"), axis=0, tiled=True),
        lax.all_gather(qkv_weight, ("gx", "gy"), axis=0, tiled=True),
        lax.all_gather(qv_bias, ("gx", "gy"), axis=1, tiled=True),
        lax.all_gather(out_weight, ("gx", "gy"), axis=0, tiled=True),
        lax.all_gather(out_bias, ("gx", "gy"), axis=0, tiled=True),
        lax.all_gather(ln2_gain, ("gx", "gy"), axis=0, tiled=True),
        lax.all_gather(ln2_shift, ("gx", "gy"), axis=0, tiled=True),
        lax.all_gather(up_weight, ("gx", "gy"), axis=0, tiled=True),
        lax.all_gather(up_bias, ("gx", "gy"), axis=0, tiled=True),
        lax.all_gather(down_weight, ("gx", "gy"), axis=0, tiled=True),
        lax.all_gather(down_bias, ("gx", "gy"), axis=0, tiled=True),
    )
    qkv_back = refetch[2]
    out_back = refetch[4]
    up_back = refetch[8]
    down_back = refetch[10]
    upstream = rows_grad.astype(jnp.float32)
    grad_down_weight = trans_dot(active, rows_grad)
    grad_down_bias = jnp.sum(upstream, axis=0)
    grad_active = back_dot(rows_grad, down_back)
    grad_hidden = gelu_pull(grad_active)[0].astype(jnp.bfloat16)
    grad_up_weight = trans_dot(normed_two, grad_hidden)
    grad_up_bias = jnp.sum(grad_hidden.astype(jnp.float32), axis=0)
    grad_normed_two = back_dot(grad_hidden, up_back)
    grad_mid_norm, grad_gain_two, grad_shift_two = norm_two_pull(grad_normed_two)
    grad_middle = upstream + grad_mid_norm
    grad_branch = grad_middle.astype(jnp.bfloat16)
    grad_out_weight = trans_dot(context, grad_branch)
    grad_out_bias = jnp.sum(grad_branch.astype(jnp.float32), axis=0)
    grad_context = back_dot(grad_branch, out_back).astype(jnp.bfloat16)
    grad_query_b, grad_key_b, grad_value_b = lax.map(
        attend_backward,
        (
            query_blocks,
            key_blocks,
            value_blocks,
            label_blocks,
            log_totals,
            grad_context.reshape(head_shape),
        ),
    )
    grad_query = grad_query_b.reshape(total_rows, model_width)
    grad_value = grad_value_b.reshape(total_rows, model_width)
    grad_joined = jnp.concatenate(
        [grad_query, grad_key_b.reshape(total_rows, model_width), grad_value], axis=1
    )
    grad_qkv_weight = trans_dot(normed, grad_joined)
    grad_qv_bias = jnp.stack(
        [
            jnp.sum(grad_query.astype(jnp.float32), axis=0),
            jnp.sum(grad_value.astype(jnp.float32), axis=0),
        ]
    )
    grad_normed = back_dot(grad_joined, qkv_back)
    grad_in_norm, grad_gain_one, grad_shift_one = norm_one_pull(grad_normed)
    input_grads = (grad_middle + grad_in_norm).astype(jnp.bfloat16)
    summed = (
        lax.psum_scatter(grad_gain_one, ("gx", "gy"), scatter_dimension=0, tiled=True),
        lax.psum_scatter(grad_shift_one, ("gx", "gy"), scatter_dimension=0, tiled=True),
        lax.psum_scatter(grad_qkv_weight, ("gx", "gy"), scatter_dimension=0, tiled=True),
        lax.psum_scatter(grad_qv_bias, ("gx", "gy"), scatter_dimension=1, tiled=True),
        lax.psum_scatter(grad_out_weight, ("gx", "gy"), scatter_dimension=0, tiled=True),
        lax.psum_scatter(grad_out_bias, ("gx", "gy"), scatter_dimension=0, tiled=True),
        lax.psum_scatter(grad_gain_two, ("gx", "gy"), scatter_dimension=0, tiled=True),
        lax.psum_scatter(grad_shift_two, ("gx", "gy"), scatter_dimension=0, tiled=True),
        lax.psum_scatter(grad_up_weight, ("gx", "gy"), scatter_dimension=0, tiled=True),
        lax.psum_scatter(grad_up_bias, ("gx", "gy"), scatter_dimension=0, tiled=True),
        lax.psum_scatter(grad_down_weight, ("gx", "gy"), scatter_dimension=0, tiled=True),
        lax.psum_scatter(grad_down_bias, ("gx", "gy"), scatter_dimension=0, tiled=True),
    )
    back_rows, back_grads = (
        lax.all_to_all(
            output_rows.reshape(gy_count, slot_capacity, model_width),
            "gy",
            split_axis=0,
            concat_axis=0,
            tiled=True,
        ),
        lax.all_to_all(
            input_grads.reshape(gy_count, slot_capacity, model_width),
            "gy",
            split_axis=0,
            concat_axis=0,
            tiled=True,
        ),
    )
    pick_rows = jnp.where(target < gy_count * slot_capacity, target, 0)
    out_flat = back_rows.reshape(-1, model_width)[pick_rows]
    grad_flat = back_grads.reshape(-1, model_width)[pick_rows]
    zero_value = jnp.zeros((), jnp.bfloat16)
    out_tokens = jnp.where(visible[:, None], out_flat, zero_value).reshape(
        samples, patches, model_width
    )
    grad_tokens = jnp.where(visible[:, None], grad_flat, zero_value).reshape(
        samples, patches, model_width
    )
    return (
        out_tokens,
        grad_tokens,
        summed[0],
        summed[1],
        summed[2],
        summed[3],
        summed[4],
        summed[5],
        summed[6],
        summed[7],
        summed[8],
        summed[9],
        summed[10],
        summed[11],
    )


def solution(mesh):
    placed = (
        P(("gx", "gy"), None, None),
        P(("gx", "gy"), None),
        P(),
        P(("gx", "gy")),
        P(("gx", "gy")),
        P(("gx", "gy"), None),
        P(None, ("gx", "gy")),
        P(("gx", "gy"), None),
        P(("gx", "gy")),
        P(("gx", "gy")),
        P(("gx", "gy")),
        P(("gx", "gy"), None),
        P(("gx", "gy")),
        P(("gx", "gy"), None),
        P(("gx", "gy")),
        P(("gx", "gy"), None, None),
    )
    return jax.shard_map(
        per_device,
        mesh=mesh,
        in_specs=placed,
        out_specs=(
            P(("gx", "gy"), None, None),
            P(("gx", "gy"), None, None),
            P(("gx", "gy")),
            P(("gx", "gy")),
            P(("gx", "gy"), None),
            P(None, ("gx", "gy")),
            P(("gx", "gy"), None),
            P(("gx", "gy")),
            P(("gx", "gy")),
            P(("gx", "gy")),
            P(("gx", "gy"), None),
            P(("gx", "gy")),
            P(("gx", "gy"), None),
            P(("gx", "gy")),
        ),
        check_vma=False,
    )
```

profile of v0, /device:TPU:0, one launch (start us, length us, event | category | flops | bytes accessed | tf_op | source)
XLA Modules:
  0.0 817.2 jit_solution(12421396141200844601)
XLA Ops:
  14.1 6.8 scatter_custom_fusion
  20.9 4.2 all-to-all-start
  28.0 50.0 %all-reduce.16 = (bf16[768]{0:T(1024)(128)(2,1)S(1)}, bf16[768]{0:T(1024)(128)(2,1)S(1)}, bf16[768]{0:T(1024)(128)(2,1)S(1)}, bf16[768]{0:T(1024)(128)(2,1)S(1)}...) all-reduce(bf16[768]{0:T(1024)(128)(2,1)S(1)} %dynamic-update-slice, ...), channel_id=1, replica_groups=mesh['gx'=8,'gy'=4] {'gx','gy'}, use_global_device_ids=true, to_apply=%add.1 | all-reduce | flops 7680 | bytes 30720
  78.7 39.2 %all-gather = bf16[32,24,2]{1,2,0:T(2,128)(2,1)S(1)} all-gather(bf16[1,24,2]{1,2,0:T(2,128)(2,1)S(1)} %bitcast.214), channel_id=1, replica_groups=mesh['gx'=8,'gy'=4] {'gx','gy'}, dimensions={0}, use_global_device_ids=true | all-gather | bytes 3168 | tf_op jit(solution)/shard_map/all_gather | solution.py:114
  118.2 6.9 scatter_custom_fusion.1
  125.1 4.3 all-to-all-start.2
  131.1 5.3 fusion.81
  139.0 3.2 reshape.602
  142.2 3.8 copy.114
  146.0 4.7 reshape.603
  150.7 4.8 copy.115
  155.5 4.7 reshape.601
  160.2 4.8 copy.112
  166.3 21.5 %while.26 = (s32[]{:T(128)}, bf16[4,1,192,12,64]{2,4,3,1,0:T(8,128)(2,1)}, f32[4,1,12,192]{3,2,1,0:T(8,128)}, bf16[4,1,192,12,64]{2,4,3,1,0:T(8,128)(2,1)}, s32[...) while((s32[]{:T(128)}, ...), condition=%wide.region_10.11_spmd, body=%wide.region_7.10_spmd.sunk | while | flops 118736640 | bytes 7126373 | solution.py:219
  168.6 2.5 fusion.128
  173.9 2.5 fusion.128
  179.3 2.5 fusion.128
  184.7 2.5 fusion.128
  187.8 4.4 copy.116
  192.2 4.0 reshape.536
  196.2 2.9 fusion.80
  199.6 9.1 %fusion.75 = f32[768,3072]{1,0:T(8,128)} fusion(bf16[768,3072]{1,0:T(8,128)(2,1)} %all-gather.10.cloned.1.call-done, f32[768,768]{1,0:T(8,128)S(1)} %get-tuple-element.274, f32[768]{0:T(1024)S(1)} %convert_element_type.144, f32[768]{0:T(1024)S(1)} %convert_element_type.143, f32[768]{0:T(1024)S(1)} %fusion.72, f32[768]{0:T(1024)S(1)} %broadcast_multiply_fusion), kind=kOutput, calls=%fused_computation.160 | convolution fusion | flops 3626827776 | bytes 16527360 | tf_op jit(solution)/shard_map/dot_general | solution.py:232
  208.7 52.0 %all-gather.12.cloned.1.call-done = bf16[3072,768]{1,0:T(8,128)(2,1)} async-done(((bf16[96,768]{1,0:T(8,128)(2,1)}), bf16[3072,768]{1,0:T(8,128)(2,1)}) %all-gather.12.cloned.1.call-update) | async-done | bytes 4718608 | tf_op jit(solution)/shard_map/all_gather | solution.py:121
  260.7 31.3 %convert_reduce_fusion = (f32[3072]{0:T(1024)}, bf16[768,3072]{1,0:T(8,128)(2,1)S(1)}, f32[768,3072]{1,0:T(8,128)}) fusion(f32[768,3072]{1,0:T(8,128)} %fusion.75, f32[3072]{0:T(1024)S(1)} %copy-done.27, bf16[768,768]{1,0:T(8,128)(2,1)} %bitcast.38, bf16[3072,768]{1,0:T(8,128)(2,1)} %all-gather.12.cloned.1.call-done), kind=kOutput, calls=%fused_computation.67 | convolution fusion | flops 3800822784 | bytes 29515776 | tf_op jit(solution)/shard_map/dot_general | solution.py:29
  292.0 4.8 multiply_reduce_fusion.1
  297.8 2.6 convert_reduce_fusion.5
  300.4 2.5 fusion.83
  304.2 2.1 convolution_convert_fusion.2
  306.3 3.6 reshape.598
  309.9 3.2 copy.121
  317.0 37.1 %while.27 = (s32[]{:T(128)}, bf16[4,1,192,12,64]{2,4,3,1,0:T(8,128)(2,1)}, bf16[4,1,192,12,64]{2,4,3,1,0:T(8,128)(2,1)}, bf16[4,1,192,12,64]{2,4,3,1,0:T(8,128)(...) while((s32[]{:T(128)}, ...), condition=%wide.region_18.19_spmd, body=%wide.region_16.18_spmd.sunk | while | flops 287868672 | bytes 18529660 | solution.py:275
  318.6 1.6 fusion.137
  321.7 2.3 fusion.140
  327.8 1.6 fusion.137
  330.9 2.3 fusion.140
  337.1 1.6 fusion.137
  340.2 2.3 fusion.140
  346.4 1.6 fusion.137
  349.5 2.3 fusion.140
  354.2 2.8 copy.124
  356.9 2.2 reshape.544
  359.2 2.4 copy.123
  361.5 4.0 reshape.543
  366.8 2.2 reshape.545
  370.9 1.7 copy-done.17
  372.6 5.2 fusion.82
  377.9 1.6 copy-done.8
  379.5 9.0 %fusion.74 = f32[768,3072]{1,0:T(8,128)} fusion(bf16[768,3072]{1,0:T(8,128)(2,1)} %copy-done.13, f32[768,768]{1,0:T(8,128)S(1)} %copy-done.8, f32[768]{0:T(1024)S(1)} %copy-done.19, f32[768]{0:T(1024)S(1)} %convert_element_type.143, f32[768]{0:T(1024)S(1)} %fusion.72, f32[768]{0:T(1024)S(1)} %broadcast_multiply_fusion), kind=kOutput, calls=%fused_computation.159 | convolution fusion | flops 3626827776 | bytes 16527360 | tf_op jit(solution)/shard_map/dot_general | solution.py:23
  389.2 11.0 %multiply_convert_fusion.1 = bf16[768,3072]{1,0:T(8,128)(2,1)} fusion(f32[768,3072]{1,0:T(8,128)} %get-tuple-element.256, f32[768,3072]{1,0:T(8,128)} %fusion.75, f32[3072]{0:T(1024)S(1)} %copy-done.28), kind=kLoop, calls=%fused_computation.69 | loop fusion | flops 9437184 | bytes 23605248 | tf_op jit(solution)/shard_map/convert_element_type | solution.py:236
  400.2 10.2 %fusion.84 = f32[3072,768]{1,0:T(8,128)} fusion(bf16[768,3072]{1,0:T(8,128)(2,1)} %multiply_convert_fusion.1, bf16[768,768]{1,0:T(8,128)(2,1)} %bitcast.38), kind=kOutput, calls=%fused_computation.167 | convolution fusion | flops 3623878656 | bytes 15335424 | tf_op jit(solution)/shard_map/dot_general | solution.py:23
  411.1 8.9 %add_convert_fusion.2 = bf16[768,768]{1,0:T(8,128)(2,1)} fusion(f32[768,768]{1,0:T(8,128)S(1)} %copy-done.8, bf16[768,3072]{1,0:T(8,128)(2,1)} %multiply_convert_fusion.1, bf16[3072,768]{1,0:T(8,128)(2,1)} %all-gather.12.cloned.1.call-done, f32[768]{0:T(1024)S(1)} %convert_element_type.148), kind=kOutput, calls=%fused_computation.114 | convolution fusion | flops 3625648128 | bytes 12979200 | tf_op jit(solution)/shard_map/dot_general | solution.py:239
  420.0 3.9 all-to-all-start.1
  423.9 6.7 fusion.76
  432.4 3.1 add_convert_fusion.1
  435.5 4.2 all-to-all-done.1
  439.7 3.5 all-to-all-start.3
  444.8 2.6 convert_reduce_fusion.1
  447.6 45.9 %all-reduce.15 = (f32[768]{0:T(1024)S(1)}, f32[768]{0:T(1024)S(1)}, f32[2,768]{1,0:T(2,128)S(1)}, f32[768]{0:T(1024)S(1)}, f32[768]{0:T(1024)S(1)}, /*index=5*/f...) all-reduce(f32[768]{0:T(1024)S(1)} %get-tuple-element.198, ...), channel_id=2, replica_groups=mesh['gx'=8,'gy'=4] {'gx','gy'}, use_global_device_ids=true, to_apply=%region_22.23.clone | all-reduce | flops 9216 | bytes 73728
  498.2 5.2 gather_fusion
  503.4 5.2 gather_fusion.1
  508.6 3.8 broadcast_select_fusion
  512.5 14.1 %reduce-scatter.6.cloned.1.call-done = f32[24,2304]{1,0:T(8,128)} async-done(((f32[768,2304]{1,0:T(8,128)}), f32[24,2304]{1,0:T(8,128)}) %reduce-scatter.6.cloned.1.call-update) | async-done | bytes 221200 | tf_op jit(solution)/shard_map/reduce_scatter | solution.py:304
  526.6 141.3 %reduce-scatter.10.cloned.1.call-done = f32[24,3072]{1,0:T(8,128)} async-done(((f32[768,3072]{1,0:T(8,128)}), f32[24,3072]{1,0:T(8,128)}) %reduce-scatter.10.cloned.1.call-update) | async-done | bytes 294928 | tf_op jit(solution)/shard_map/reduce_scatter | solution.py:310
  667.9 142.1 %reduce-scatter.12.cloned.1.call-done = f32[96,768]{1,0:T(8,128)} async-done(((f32[3072,768]{1,0:T(8,128)}), f32[96,768]{1,0:T(8,128)}) %reduce-scatter.12.cloned.1.call-update) | async-done | bytes 294928 | tf_op jit(solution)/shard_map/reduce_scatter | solution.py:312
  (249 shorter events, 67.9 us)
Async XLA Ops:
  7.2 18.5 %copy-start.37 = (s32[256]{0:T(256)S(1)}, s32[256]{0:T(256)}, u32[]{:S(2)}) copy-start(s32[256]{0:T(256)} %param.22) | copy-start | bytes 3076
  7.2 19.1 %copy-start.40 = (bf16[24]{0:T(256)(128)(2,1)S(1)}, bf16[24]{0:T(256)(128)(2,1)}, u32[]{:S(2)}) copy-start(bf16[24]{0:T(256)(128)(2,1)} %param.29) | copy-start | bytes 148
  7.2 19.4 %copy-start.41 = (bf16[24]{0:T(256)(128)(2,1)S(1)}, bf16[24]{0:T(256)(128)(2,1)}, u32[]{:S(2)}) copy-start(bf16[24]{0:T(256)(128)(2,1)} %param.30) | copy-start | bytes 148
  7.2 19.6 %copy-start.42 = (bf16[24]{0:T(256)(128)(2,1)S(1)}, bf16[24]{0:T(256)(128)(2,1)}, u32[]{:S(2)}) copy-start(bf16[24]{0:T(256)(128)(2,1)} %param.28) | copy-start | bytes 148
  7.2 19.8 %copy-start.43 = (bf16[24]{0:T(256)(128)(2,1)S(1)}, bf16[24]{0:T(256)(128)(2,1)}, u32[]{:S(2)}) copy-start(bf16[24]{0:T(256)(128)(2,1)} %param.23) | copy-start | bytes 148
  7.2 20.1 %copy-start.44 = (bf16[24]{0:T(256)(128)(2,1)S(1)}, bf16[24]{0:T(256)(128)(2,1)}, u32[]{:S(2)}) copy-start(bf16[24]{0:T(256)(128)(2,1)} %param.24) | copy-start | bytes 148
  7.2 20.3 %copy-start.45 = (bf16[24]{0:T(256)(128)(2,1)S(1)}, bf16[24]{0:T(256)(128)(2,1)}, u32[]{:S(2)}) copy-start(bf16[24]{0:T(256)(128)(2,1)} %param.34) | copy-start | bytes 148
  7.3 20.5 %copy-start.46 = (bf16[96]{0:T(256)(128)(2,1)S(1)}, bf16[96]{0:T(256)(128)(2,1)}, u32[]{:S(2)}) copy-start(bf16[96]{0:T(256)(128)(2,1)} %param.32) | copy-start | bytes 580
  7.3 71.4 %copy-start.36 = (bf16[2,24]{1,0:T(2,128)(2,1)S(1)}, bf16[2,24]{1,0:T(2,128)(2,1)}, u32[]{:S(2)}) copy-start(bf16[2,24]{1,0:T(2,128)(2,1)} %param.26) | copy-start | bytes 292
  7.3 123.8 %all-gather.6.cloned.1.call-start = ((), (), s32[]{:S(2)}) async-start(), calls=%async_computation.8 | async-start | bytes 3649536 | tf_op jit(solution)/shard_map/all_gather | solution.py:113
  8.0 188.2 %all-gather.8.cloned.1.call-start = ((), (), s32[]{:S(2)}) async-start(), calls=%async_computation.9 | async-start | bytes 1216512 | tf_op jit(solution)/shard_map/all_gather | solution.py:115
  8.8 190.8 %all-gather.10.cloned.1.call-start = ((), (), s32[]{:S(2)}) async-start(), calls=%async_computation.10 | async-start | bytes 4866048 | tf_op jit(solution)/shard_map/all_gather | solution.py:119
  20.9 104.1 %all-to-all-start = ((bf16[4,192,768]{2,1,0:T(8,128)(2,1)}), bf16[4,192,768]{2,1,0:T(8,128)(2,1)S(1)}, u32[]{:S(2)}, u32[]{:S(2)}) async-start(bf16[4,192,768]{2,1,0:T(8,128)(2,1)} %bitcast.26), calls=%async_computation | async-start | bytes 2359296 | tf_op jit(solution)/shard_map/all_to_all | solution.py:150
  25.1 235.6 %all-gather.12.cloned.1.call-start = ((), (), s32[]{:S(2)}) async-start(), calls=%async_computation.11 | async-start | bytes 4866048 | tf_op jit(solution)/shard_map/all_gather | solution.py:121
  78.1 52.5 %copy-start.20 = (f32[768]{0:T(1024)}, f32[768]{0:T(1024)S(1)}, u32[]{:S(2)}) copy-start(f32[768]{0:T(1024)S(1)} %convert_element_type.136) | copy-start | bytes 9220
  78.1 121.5 %copy-start.18 = (f32[768]{0:T(1024)}, f32[768]{0:T(1024)S(1)}, u32[]{:S(2)}) copy-start(f32[768]{0:T(1024)S(1)} %convert_element_type.144) | copy-start | bytes 9220
  125.1 71.2 %copy-start = (bf16[4,192,768]{2,1,0:T(8,128)(2,1)}, bf16[4,192,768]{2,1,0:T(8,128)(2,1)S(1)}, u32[]{:S(2)}) copy-start(bf16[4,192,768]{2,1,0:T(8,128)(2,1)S(1)} %all-to-all-done) | copy-start | bytes 3538948
  125.1 83.7 %all-to-all-start.2 = ((bf16[4,192,768]{2,1,0:T(8,128)(2,1)}), bf16[4,192,768]{2,1,0:T(8,128)(2,1)}, u32[]{:S(2)}, u32[]{:S(2)}) async-start(bf16[4,192,768]{2,1,0:T(8,128)(2,1)} %bitcast.37), calls=%async_computation.2 | async-start | bytes 2359296 | tf_op jit(solution)/shard_map/all_to_all | solution.py:157
  129.4 383.1 %reduce-scatter.8.cloned.1.call-start = ((), (), s32[]{:S(2)}) async-start(), calls=%async_computation.13 | async-start | bytes 2433024 | tf_op jit(solution)/shard_map/reduce_scatter | solution.py:306
  129.9 6.5 copy-start.22
  130.5 5.9 copy-start.29
  130.5 5.9 copy-start.24
  131.0 5.4 copy-start.14
  187.8 8.4 %copy-start.2 = (bf16[4,1,192,12,64]{2,4,3,1,0:T(8,128)(2,1)}, bf16[4,1,192,12,64]{2,4,3,1,0:T(8,128)(2,1)S(1)}, u32[]{:S(2)}) copy-start(bf16[4,1,192,12,64]{2,4,3,1,0:T(8,128)(2,1)S(1)} %get-tuple-element.461) | copy-start | bytes 3538948
  187.8 8.4 %copy-start.26 = (s32[4,1,192]{2,1,0:T(1,128)}, s32[4,1,192]{2,1,0:T(1,128)S(1)}, u32[]{:S(2)}) copy-start(s32[4,1,192]{2,1,0:T(1,128)S(1)} %get-tuple-element.476) | copy-start | bytes 9220
  199.1 97.7 %copy-start.7 = (f32[768,768]{1,0:T(8,128)}, f32[768,768]{1,0:T(8,128)S(1)}, u32[]{:S(2)}) copy-start(f32[768,768]{1,0:T(8,128)S(1)} %get-tuple-element.274) | copy-start | bytes 7077892
  199.5 61.2 %copy-start.27 = (f32[3072]{0:T(1024)S(1)}, f32[3072]{0:T(1024)}, u32[]{:S(2)}) copy-start(f32[3072]{0:T(1024)} %convert_element_type.146) | copy-start | bytes 36868
  260.7 31.3 %copy-start.38 = (bf16[768,3072]{1,0:T(8,128)(2,1)S(1)}, bf16[768,3072]{1,0:T(8,128)(2,1)}, u32[]{:S(2)}) copy-start(bf16[768,3072]{1,0:T(8,128)(2,1)} %all-gather.10.cloned.1.call-done) | copy-start | bytes 14155780
  292.0 4.8 copy-start.13
  297.7 2.6 copy-start.5
  297.8 2.6 copy-start.16
  302.9 1.3 copy-start.39
  302.9 223.7 %reduce-scatter.6.cloned.1.call-start = ((), (), s32[]{:S(2)}) async-start(), calls=%async_computation.12 | async-start | bytes 7299072 | tf_op jit(solution)/shard_map/reduce_scatter | solution.py:304
  313.0 4.0 copy-start.3
  313.0 4.0 copy-start.4
  354.2 5.0 copy-start.10
  359.2 6.4 copy-start.9
  366.8 3.8 copy-start.11
  369.0 1.8 copy-start.12
  370.6 2.0 copy-start.15
  370.9 1.7 copy-start.17
  377.8 1.7 copy-start.8
  377.8 1.7 copy-start.19
  377.8 290.0 %reduce-scatter.10.cloned.1.call-start = ((), (), s32[]{:S(2)}) async-start(), calls=%async_computation.14 | async-start | bytes 9732096 | tf_op jit(solution)/shard_map/reduce_scatter | solution.py:310
  388.5 0.7 copy-start.28
  388.6 421.4 %reduce-scatter.12.cloned.1.call-start = ((), (), s32[]{:S(2)}) async-start(), calls=%async_computation.15 | async-start | bytes 9732096 | tf_op jit(solution)/shard_map/reduce_scatter | solution.py:312
  410.4 0.6 copy-start.35
  420.0 3.9 copy-start.1
  420.0 3.9 copy-start.21
  420.0 4.0 copy-start.23
  420.0 19.7 %all-to-all-start.1 = ((bf16[4,192,768]{2,1,0:T(8,128)(2,1)}), bf16[4,192,768]{2,1,0:T(8,128)(2,1)S(1)}, u32[]{:S(2)}, u32[]{:S(2)}) async-start(bf16[4,192,768]{2,1,0:T(8,128)(2,1)} %bitcast.32), calls=%async_computation.1 | async-start | bytes 2359296 | tf_op jit(solution)/shard_map/all_to_all | solution.py:316
  423.9 6.8 copy-start.30
  423.9 6.8 copy-start.25
  430.7 1.7 copy-start.6
  435.5 7.8 copy-start.31
  439.7 63.7 %all-to-all-start.3 = ((bf16[4,192,768]{2,1,0:T(8,128)(2,1)}), bf16[4,192,768]{2,1,0:T(8,128)(2,1)S(1)}, u32[]{:S(2)}, u32[]{:S(2)}) async-start(bf16[4,192,768]{2,1,0:T(8,128)(2,1)} %bitcast.39), calls=%async_computation.3 | async-start | bytes 2359296 | tf_op jit(solution)/shard_map/all_to_all | solution.py:323
  443.2 4.3 copy-start.32
  443.3 4.3 copy-start.33
  503.4 5.2 copy-start.34
Sparse Core Ops, SparseCore 0:
  11.0 63.1 all-gather.5
  77.1 52.7 all-gather.7
  132.8 62.5 all-gather.9
  198.2 62.4 all-gather.11
  303.0 97.8 reduce-scatter.7
  408.0 118.5 reduce-scatter.5
  533.1 134.7 reduce-scatter.9
  675.3 134.5 reduce-scatter.11
where the time goes:
time: 827 us; the launch traced here: 817 us
  waiting for transfers between devices  356 us (43%)
  matrix products  144 us (17%)
  blocking collectives  135 us (16%)
  local copies, waits for them, and re-layouts  109 us (13%)
  other arithmetic  41.6 us (5%)
  starting transfers between devices  16.5 us (2%)
  between operations  15.3 us (2%)
    reduce_scatter x1, waiting for transfers between devices, per_device(): lax.psum_scatter(grad_down_weight, ('gx', 'gy'), scatter_dimension=0, til...  142 us
    reduce_scatter x1, waiting for transfers between devices, per_device(): lax.psum_scatter(grad_up_weight, ('gx', 'gy'), scatter_dimension=0, tiled...  141 us
    unnamed x2, blocking collectives  95.9 us
    all_gather x1, waiting for transfers between devices, per_device(): lax.all_gather(down_weight, ('gx', 'gy'), axis=0, tiled=True)  52 us
    dot_general x4, matrix products, back_dot(): lax.dot_general(left, right, (((1,), (1,)), ((), ())), preferred_element_...  45 us
    all_gather x1, blocking collectives, per_device(): lax.all_gather(qv_bias, ('gx', 'gy'), axis=1, tiled=True)  39.2 us
    dot_general x4, matrix products, trans_dot(): lax.dot_general(left, right, (((0,), (0,)), ((), ())), preferred_element_...  27 us
    while x5, local copies, waits for them, and re-layouts, per_device(): lax.map(attend_forward, (query_blocks, key_blocks, value_blocks, label_bl...  17.7 us
  transfers between devices with their start and end apart: 12, of which 5 were waited for; matrix products, arithmetic and copies ran while one was open for 30% of the time, Pallas kernels for 0%

commit v1 on v0

--- a/solution.py
+++ b/solution.py
@@ -1,12 +1,543 @@
+import functools
 import math
 
 import jax
 import jax.numpy as jnp
 from jax import lax
+from jax.experimental import pallas as pl
+from jax.experimental.pallas import tpu as pltpu
 from jax.sharding import PartitionSpec as P
 
 HEADS = 12
 HD = 64
+MESH = pl.DeviceIdType.MESH
+
+
+class Place:
+    def __init__(self, chain):
+        gx = lax.axis_index("gx")
+        gy = lax.axis_index("gy")
+        self.chain = chain
+        self.a = gx // 2
+        self.b = gx % 2
+        self.c = gy // 2
+        self.d = gy % 2
+
+    def shard(self, a=None, b=None, c=None, d=None):
+        a = self.a if a is None else a
+        b = self.b if b is None else b
+        c = self.c if c is None else c
+        d = self.d if d is None else d
+        return ((a * 2 + b) * 2 + c) * 2 + d
+
+    def device(self, a=None, b=None, c=None, d=None):
+        a = self.a if a is None else a
+        b = self.b if b is None else b
+        c = self.c if c is None else c
+        d = self.d if d is None else d
+        return (a * 2 + b, c * 2 + d)
+
+    def greet(self):
+        barrier = pltpu.get_barrier_semaphore()
+        has_below = self.a > 0
+        has_above = self.a < self.chain - 1
+        for to in (
+            self.device(d=1 - self.d),
+            self.device(c=1 - self.c),
+            self.device(b=1 - self.b),
+        ):
+            pl.semaphore_signal(barrier, inc=1, device_id=to, device_id_type=MESH)
+
+        @pl.when(has_below)
+        def _():
+            pl.semaphore_signal(
+                barrier, inc=1, device_id=self.device(a=self.a - 1), device_id_type=MESH
+            )
+
+        @pl.when(has_above)
+        def _():
+            pl.semaphore_signal(
+                barrier, inc=1, device_id=self.device(a=self.a + 1), device_id_type=MESH
+            )
+
+        pl.semaphore_wait(
+            barrier, 3 + has_below.astype(jnp.int32) + has_above.astype(jnp.int32)
+        )
+
+
+def halves(widths):
+    parts = []
+    for at, width in enumerate(widths):
+        if width % 256:
+            parts.append((at, 0, width, "b"))
+        else:
+            parts.append((at, 0, width // 2, "b"))
+            parts.append((at, width // 2, width // 2, "c"))
+    return parts
+
+
+class Gather:
+    def __init__(self, place, parts, own, full, sems):
+        self.place, self.parts, self.own, self.full = place, parts, own, full
+        self.chain_sem, self.send_sem, self.recv_sem = sems
+
+    def view(self, part, index):
+        at, first, width, _ = self.parts[part]
+        return self.full[at].at[index, :, pl.ds(first, width)]
+
+    def copy(self, part, index, to, send, own=False):
+        at, first, width, _ = self.parts[part]
+        src = self.own[at].at[:, pl.ds(first, width)] if own else self.view(part, index)
+        return pltpu.make_async_remote_copy(
+            src_ref=src,
+            dst_ref=self.view(part, index),
+            send_sem=send,
+            recv_sem=self.recv_sem.at[part, index],
+            device_id=to,
+            device_id_type=MESH,
+        )
+
+    def flip(self, axis):
+        place = self.place
+        return {axis: 1 - {"b": place.b, "c": place.c, "d": place.d}[axis]}
+
+    def links(self, part):
+        first = self.parts[part][3]
+        return first, ("c" if first == "b" else "b")
+
+    def send_pair(self, part, index, axis, own=False):
+        self.copy(part, index, self.place.device(**self.flip(axis)), self.send_sem.at[part], own).start()
+
+    def arrived(self, part, index):
+        self.copy(part, index, self.place.device(d=1 - self.place.d), self.send_sem.at[part]).wait_recv()
+
+    def begin(self, part):
+        place = self.place
+        mine = place.shard()
+        first, second = self.links(part)
+
+        @pl.when(place.a < place.chain - 1)
+        def _():
+            self.copy(part, mine, place.device(a=place.a + 1), self.chain_sem.at[part, 0, 0], True).start()
+
+        @pl.when(place.a > 0)
+        def _():
+            self.copy(part, mine, place.device(a=place.a - 1), self.chain_sem.at[part, 1, 0], True).start()
+
+        for axis in (first, second, "d"):
+            self.send_pair(part, mine, axis, True)
+
+    def chain_step(self, part, step):
+        place = self.place
+        first, second = self.links(part)
+
+        @pl.when(place.a - 1 - step >= 0)
+        def _():
+            index = place.shard(a=place.a - 1 - step)
+            self.arrived(part, index)
+
+            @pl.when(place.a < place.chain - 1)
+            def _():
+                self.copy(
+                    part, index, place.device(a=place.a + 1), self.chain_sem.at[part, 0, step + 1]
+                ).start()
+
+            for axis in (first, second, "d"):
+                self.send_pair(part, index, axis)
+
+        @pl.when(place.a + 1 + step < place.chain)
+        def _():
+            index = place.shard(a=place.a + 1 + step)
+            self.arrived(part, index)
+
+            @pl.when(place.a > 0)
+            def _():
+                self.copy(
+                    part, index, place.device(a=place.a - 1), self.chain_sem.at[part, 1, step + 1]
+                ).start()
+
+            for axis in (first, second, "d"):
+                self.send_pair(part, index, axis)
+
+    def cross_one(self, part, row):
+        place = self.place
+        first, second = self.links(part)
+        index = place.shard(a=row, **self.flip(first))
+        self.arrived(part, index)
+        for axis in (second, "d"):
+            self.send_pair(part, index, axis)
+
+    def cross_step(self, part, step):
+        place = self.place
+        if isinstance(step, int) and step == 0:
+            self.cross_one(part, place.a)
+            return
+
+        @pl.when(place.a - step >= 0)
+        def _():
+            self.cross_one(part, place.a - step)
+
+        @pl.when(place.a + step < place.chain)
+        def _():
+            self.cross_one(part, place.a + step)
+
+    def last_one(self, part, row, other):
+        place = self.place
+        first, second = self.links(part)
+        where = self.flip(second)
+        if other:
+            where.update(self.flip(first))
+        index = place.shard(a=row, **where)
+        self.arrived(part, index)
+        self.send_pair(part, index, "d")
+
+    def last_step(self, part, step):
+        place = self.place
+        if isinstance(step, int) and step == 0:
+            for other in (False, True):
+                self.last_one(part, place.a, other)
+            return
+
+        @pl.when(place.a - step >= 0)
+        def _():
+            for other in (False, True):
+                self.last_one(part, place.a - step, other)
+
+        @pl.when(place.a + step < place.chain)
+        def _():
+            for other in (False, True):
+                self.last_one(part, place.a + step, other)
+
+    def finish(self, part):
+        place = self.place
+
+        def one(at, carry):
+            self.arrived(part, at * 2 + 1 - place.d)
+            return carry
+
+        lax.fori_loop(0, 4 * place.chain, one, 0)
+        at, first, width, _ = self.parts[part]
+        block = self.full[at].at[pl.ds(0, 7 * place.chain), :, pl.ds(first, width)]
+        pltpu.make_async_copy(block, block, self.send_sem.at[part]).wait()
+
+        def sent(step, carry):
+            @pl.when((place.a < place.chain - 1) & (place.a - step >= 0))
+            def _():
+                self.copy(
+                    part, place.shard(a=place.a - step), place.device(a=place.a + 1), self.chain_sem.at[part, 0, step]
+                ).wait_send()
+
+            @pl.when((place.a > 0) & (place.a + step < place.chain))
+            def _():
+                self.copy(
+                    part, place.shard(a=place.a + step), place.device(a=place.a - 1), self.chain_sem.at[part, 1, step]
+                ).wait_send()
+
+            return carry
+
+        lax.fori_loop(0, place.chain - 1, sent, 0)
+
+
+def gather_kernel(chain, parts, count, *refs):
+    own, full = refs[:count], refs[count : 2 * count]
+    chain_sem, send_sem, recv_sem, keep_sem = refs[2 * count :]
+    place = Place(chain)
+    mine = place.shard()
+    place.greet()
+    engine = Gather(place, parts, own, full, (chain_sem, send_sem, recv_sem))
+    keeps = [
+        pltpu.make_async_copy(own[at], full[at].at[mine], keep_sem.at[at]) for at in range(count)
+    ]
+    numbers = range(len(parts))
+    for part in numbers:
+        engine.begin(part)
+    for keep in keeps:
+        keep.start()
+
+    def step(at, carry):
+        for part in numbers:
+            engine.chain_step(part, at)
+
+        @pl.when(at == 0)
+        def _():
+            for part in numbers:
+                engine.cross_step(part, 0)
+
+        @pl.when(at > 0)
+        def _():
+            for part in numbers:
+                engine.cross_step(part, at)
+
+        return carry
+
+    lax.fori_loop(0, chain - 1, step, 0)
+    for part in numbers:
+        engine.cross_step(part, chain - 1)
+    for part in numbers:
+        engine.last_step(part, 0)
+
+    def last(at, carry):
+        for part in numbers:
+            engine.last_step(part, at)
+        return carry
+
+    lax.fori_loop(1, chain, last, 0)
+    for part in numbers:
+        engine.finish(part)
+    for keep in keeps:
+        keep.wait()
+
+
+def gather_all(chain, shards):
+    count = len(shards)
+    devices = 8 * chain
+    parts = halves([item.shape[1] for item in shards])
+    return pl.pallas_call(
+        functools.partial(gather_kernel, chain, parts, count),
+        out_shape=[jax.ShapeDtypeStruct((devices,) + item.shape, item.dtype) for item in shards],
+        in_specs=[pl.BlockSpec(memory_space=pl.ANY)] * count,
+        out_specs=[pl.BlockSpec(memory_space=pl.ANY)] * count,
+        scratch_shapes=[
+            pltpu.SemaphoreType.DMA((len(parts), 2, chain)),
+            pltpu.SemaphoreType.DMA((len(parts),)),
+            pltpu.SemaphoreType.DMA((len(parts), devices)),
+            pltpu.SemaphoreType.DMA((count,)),
+        ],
+        compiler_params=pltpu.CompilerParams(collective_id=0, has_side_effects=True),
+        name="gather_all",
+    )(*shards)
+
+
+class Scatter:
+    def __init__(self, place, parts, terms, got, sems):
+        self.place, self.parts, self.terms = place, parts, terms
+        self.got = got
+        self.send_sem, self.recv_sem, self.chain_send, self.chain_recv = sems
+
+    def pick(self, ref, lead, part):
+        _, first, width, _ = self.parts[part]
+        return ref.at[lead + (slice(None), pl.ds(first, width))]
+
+    def exchange(self, part, level, src, dst, to):
+        return pltpu.make_async_remote_copy(
+            src_ref=src,
+            dst_ref=dst,
+            send_sem=self.send_sem.at[part, level],
+            recv_sem=self.recv_sem.at[part, level],
+            device_id=to,
+            device_id_type=MESH,
+        )
+
+    def core(self, part):
+        place = self.place
+        at = self.parts[part][0]
+        every = slice(None)
+        return self.exchange(
+            part,
+            0,
+            self.pick(self.terms[at], (every, every, every, 1 - place.d), part),
+            self.pick(self.got[at][0], (every, every, every), part),
+            place.device(d=1 - place.d),
+        )
+
+    def lead(self, part, level, mine):
+        place = self.place
+        every = slice(None)
+        first = self.parts[part][3]
+        b = place.b if mine else 1 - place.b
+        c = place.c if mine else 1 - place.c
+        if level == 1:
+            return (every, b, every) if first == "b" else (every, every, c)
+        return (every, c) if first == "b" else (every, b)
+
+    def pair(self, part, level):
+        place = self.place
+        at, _, _, first = self.parts[part]
+        axis = first if level == 1 else ("c" if first == "b" else "b")
+        to = place.device(b=1 - place.b) if axis == "b" else place.device(c=1 - place.c)
+        every = slice(None)
+        dst = (every, every) if level == 1 else (every,)
+        return self.exchange(
+            part,
+            level,
+            self.pick(self.got[at][level - 1], self.lead(part, level, False), part),
+            self.pick(self.got[at][level], dst, part),
+            to,
+        )
+
+    def add_core(self, part):
+        place = self.place
+        at, first, width, _ = self.parts[part]
+        self.core(part).wait_recv()
+        terms, got = self.terms[at], self.got[at][0]
+        columns = pl.ds(first, width)
+
+        def one(i, carry):
+            x = i // 4
+            y = i // 2 % 2
+            z = i % 2
+            got[x, y, z, :, columns] = got[x, y, z, :, columns] + terms[x, y, z, place.d, :, columns]
+            return carry
+
+        lax.fori_loop(0, 4 * place.chain, one, 0)
+
+    def add_pair(self, part, level):
+        place = self.place
+        at, first, width, axis = self.parts[part]
+        self.pair(part, level).wait_recv()
+        before, got = self.got[at][level - 1], self.got[at][level]
+        columns = pl.ds(first, width)
+
+        def one(i, carry):
+            if level == 1:
+                x, y = i // 2, i % 2
+                if axis == "b":
+                    kept = before[x, place.b, y, :, columns]
+                else:
+                    kept = before[x, y, place.c, :, columns]
+                got[x, y, :, columns] = got[x, y, :, columns] + kept
+            else:
+                kept = before[i, place.c if axis == "b" else place.b, :, columns]
+                got[i, :, columns] = got[i, :, columns] + kept
+            return carry
+
+        lax.fori_loop(0, (2 if level == 1 else 1) * place.chain, one, 0)
+
+    def hop(self, part, way, row):
+        place = self.place
+        at = self.parts[part][0]
+        to = place.device(a=place.a + 1) if way == 0 else place.device(a=place.a - 1)
+        return pltpu.make_async_remote_copy(
+            src_ref=self.pick(self.got[at][2], (row,), part),
+            dst_ref=self.pick(self.got[at][3 + way], (row,), part),
+            send_sem=self.chain_send.at[part, row],
+            recv_sem=self.chain_recv.at[part, way, row],
+            device_id=to,
+            device_id_type=MESH,
+        )
+
+    def take(self, part, way, row):
+        place = self.place
+        at, first, width, _ = self.parts[part]
+        columns = pl.ds(first, width)
+        self.hop(part, way, row).wait_recv()
+        got = self.got[at][2]
+        got[row, :, columns] = got[row, :, columns] + self.got[at][3 + way][row, :, columns]
+
+    def chain_step(self, part, step):
+        place = self.place
+        top = place.chain - 1 - step
+
+        @pl.when(place.a < top)
+        def _():
+            @pl.when(place.a > 0)
+            def _():
+                self.take(part, 0, top)
+
+            self.hop(part, 0, top).start()
+
+        @pl.when(place.a > step)
+        def _():
+            @pl.when(place.a < place.chain - 1)
+            def _():
+                self.take(part, 1, step)
+
+            self.hop(part, 1, step).start()
+
+    def result(self, part, out):
+        place = self.place
+        at, first, width, _ = self.parts[part]
+        columns = pl.ds(first, width)
+        a = place.a
+        got = self.got[at]
+
+        def add(way):
+            self.hop(part, way, a).wait_recv()
+            out[at][:, columns] = out[at][:, columns] + got[3 + way][a, :, columns].astype(jnp.float32)
+
+        out[at][:, columns] = got[2][a, :, columns].astype(jnp.float32)
+        pl.when(a > 0)(lambda: add(0))
+        pl.when(a < place.chain - 1)(lambda: add(1))
+
+    def finish(self, part):
+        place = self.place
+        self.core(part).wait_send()
+        for level in (1, 2):
+            self.pair(part, level).wait_send()
+
+        def one(row, carry):
+            @pl.when(row > place.a)
+            def _():
+                self.hop(part, 0, row).wait_send()
+
+            @pl.when(row < place.a)
+            def _():
+                self.hop(part, 1, row).wait_send()
+
+            return carry
+
+        lax.fori_loop(0, place.chain, one, 0)
+
+
+def scatter_buffers(chain, shapes):
+    out = []
+    for rows, width, dtype in shapes:
+        for lead in ((chain, 2, 2), (chain, 2), (chain,), (chain,), (chain,)):
+            out.append(pltpu.VMEM(lead + (rows, width), dtype))
+    return out
+
+
+def scatter_kernel(chain, parts, count, *refs):
+    terms, out = refs[:count], refs[count : 2 * count]
+    buffers = refs[2 * count : 7 * count]
+    sems = refs[7 * count :]
+    got = [buffers[5 * at : 5 * at + 5] for at in range(count)]
+    place = Place(chain)
+    place.greet()
+    engine = Scatter(place, parts, terms, got, sems)
+    numbers = range(len(parts))
+    for part in numbers:
+        engine.core(part).start()
+    for part in numbers:
+        engine.add_core(part)
+        engine.pair(part, 1).start()
+    for part in numbers:
+        engine.add_pair(part, 1)
+        engine.pair(part, 2).start()
+    for part in numbers:
+        engine.add_pair(part, 2)
+
+        def step(at, carry, part=part):
+            engine.chain_step(part, at)
+            return carry
+
+        lax.fori_loop(0, chain - 1, step, 0)
+    for part in numbers:
+        engine.result(part, out)
+    for part in numbers:
+        engine.finish(part)
+
+
+def scatter_all(chain, terms):
+    count = len(terms)
+    parts = halves([item.shape[-1] for item in terms])
+    return pl.pallas_call(
+        functools.partial(scatter_kernel, chain, parts, count),
+        out_shape=[jax.ShapeDtypeStruct(item.shape[-2:], jnp.float32) for item in terms],
+        in_specs=[pl.BlockSpec(memory_space=pltpu.VMEM)] * count,
+        out_specs=[pl.BlockSpec(memory_space=pltpu.VMEM)] * count,
+        scratch_shapes=scatter_buffers(chain, [item.shape[-2:] + (item.dtype,) for item in terms])
+        + [
+            pltpu.SemaphoreType.DMA((len(parts), 3)),
+            pltpu.SemaphoreType.DMA((len(parts), 3)),
+            pltpu.SemaphoreType.DMA((len(parts), chain)),
+            pltpu.SemaphoreType.DMA((len(parts), 2, chain)),
+        ],
+        compiler_params=pltpu.CompilerParams(
+            collective_id=1, has_side_effects=True, vmem_limit_bytes=60 * 2**20
+        ),
+        name="scatter_all",
+    )(*terms)
 
 
 def layer_norm(values, gain, shift):
@@ -107,21 +638,23 @@
     down_bias,
     cotangent,
 ):
-    gathered = (
-        lax.all_gather(ln1_gain, ("gx", "gy"), axis=0, tiled=True),
-        lax.all_gather(ln1_shift, ("gx", "gy"), axis=0, tiled=True),
-        lax.all_gather(qkv_weight, ("gx", "gy"), axis=0, tiled=True),
-        lax.all_gather(qv_bias, ("gx", "gy"), axis=1, tiled=True),
-        lax.all_gather(out_weight, ("gx", "gy"), axis=0, tiled=True),
-        lax.all_gather(out_bias, ("gx", "gy"), axis=0, tiled=True),
-        lax.all_gather(ln2_gain, ("gx", "gy"), axis=0, tiled=True),
-        lax.all_gather(ln2_shift, ("gx", "gy"), axis=0, tiled=True),
-        lax.all_gather(up_weight, ("gx", "gy"), axis=0, tiled=True),
-        lax.all_gather(up_bias, ("gx", "gy"), axis=0, tiled=True),
-        lax.all_gather(down_weight, ("gx", "gy"), axis=0, tiled=True),
-        lax.all_gather(down_bias, ("gx", "gy"), axis=0, tiled=True),
-    )
+    chain = lax.axis_size("gx") // 2
+    devices = 8 * chain
     samples, patches, model_width = tokens.shape
+    small = [ln1_gain, ln1_shift, qv_bias[0], qv_bias[1], out_bias, ln2_gain, ln2_shift, down_bias, up_bias]
+    vector_rows = jnp.stack([jnp.pad(item, (0, 128 - item.shape[0])) for item in small])
+    vector_rows = jnp.pad(vector_rows, ((0, 16 - len(small)), (0, 0)))
+    qkv_all, out_all, up_all, down_all, vectors = gather_all(
+        chain, [qkv_weight, out_weight, up_weight, down_weight, vector_rows]
+    )
+    qkv_full = qkv_all.reshape(-1, qkv_weight.shape[1])
+    out_full = out_all.reshape(-1, out_weight.shape[1])
+    up_full = up_all.reshape(-1, up_weight.shape[1])
+    down_full = down_all.reshape(-1, down_weight.shape[1])
+    (gain_one, shift_one, bias_q, bias_v, bias_out, gain_two, shift_two, bias_down, bias_up) = [
+        vectors[:, at, : item.shape[0]].reshape(-1) for at, item in enumerate(small)
+    ]
+    bias_qv = jnp.stack([bias_q, bias_v])
     gy_count = lax.axis_size("gy")
     row_index = lax.axis_index("gy")
     column_index = lax.axis_index("gx")
@@ -146,59 +679,13 @@
         .at[target]
         .set(cotangent.reshape(-1, model_width), mode="drop")
     )
-    arrived_rows, arrived_grads = (
-        lax.all_to_all(
-            send_rows.reshape(gy_count, slot_capacity, model_width),
-            "gy",
-            split_axis=0,
-            concat_axis=0,
-            tiled=True,
-        ),
-        lax.all_to_all(
-            send_grads.reshape(gy_count, slot_capacity, model_width),
-            "gy",
-            split_axis=0,
-            concat_axis=0,
-            tiled=True,
-        ),
-    )
-    team_start = column_index * gy_count * samples
-    team_count = lax.dynamic_slice_in_dim(counts, team_start, gy_count * samples).reshape(
-        gy_count, samples
-    )
-    team_offset = start_rows(team_count, gy_count)
-    team_dest = jnp.broadcast_to(
-        (jnp.arange(samples, dtype=jnp.int32) % gy_count)[None, :], (gy_count, samples)
-    )
     slot_rows = jnp.arange(slot_capacity, dtype=jnp.int32)
-    member = (
-        (team_dest[:, :, None] == row_index)
-        & (slot_rows[None, None, :] >= team_offset[:, :, None])
-        & (slot_rows[None, None, :] < team_offset[:, :, None] + team_count[:, :, None])
-    )
-    label_ids = (
-        jnp.arange(gy_count, dtype=jnp.int32)[:, None] * samples
-        + jnp.arange(samples, dtype=jnp.int32)[None, :]
-        + 1
-    )
-    labels = (jnp.sum(jnp.where(member, label_ids[:, :, None], 0), axis=1) - 1).reshape(-1)
-    rows_in = arrived_rows.reshape(-1, model_width)
-    rows_grad = arrived_grads.reshape(-1, model_width)
+    first_count = own_count[:gy_count, None]
+    both_count = first_count + own_count[gy_count:, None]
+    labels = jnp.where(slot_rows < first_count, 0, jnp.where(slot_rows < both_count, 1, 2))
+    rows_in = send_rows
+    rows_grad = send_grads
     per_step = math.gcd(gy_count, max(1, -(-512 // slot_capacity)))
-    (
-        gain_one,
-        shift_one,
-        qkv_full,
-        bias_qv,
-        out_full,
-        bias_out,
-        gain_two,
-        shift_two,
-        up_full,
-        bias_up,
-        down_full,
-        bias_down,
-    ) = gathered
     total_rows = rows_in.shape[0]
     inputs = rows_in.astype(jnp.float32)
     normed_f, norm_one_pull = jax.vjp(
@@ -240,38 +727,20 @@
         + bias_down.astype(jnp.float32)
     )
     output_rows = result.astype(jnp.bfloat16)
-    refetch = (
-        lax.all_gather(ln1_gain, ("gx", "gy"), axis=0, tiled=True),
-        lax.all_gather(ln1_shift, ("gx", "gy"), axis=0, tiled=True),
-        lax.all_gather(qkv_weight, ("gx", "gy"), axis=0, tiled=True),
-        lax.all_gather(qv_bias, ("gx", "gy"), axis=1, tiled=True),
-        lax.all_gather(out_weight, ("gx", "gy"), axis=0, tiled=True),
-        lax.all_gather(out_bias, ("gx", "gy"), axis=0, tiled=True),
-        lax.all_gather(ln2_gain, ("gx", "gy"), axis=0, tiled=True),
-        lax.all_gather(ln2_shift, ("gx", "gy"), axis=0, tiled=True),
-        lax.all_gather(up_weight, ("gx", "gy"), axis=0, tiled=True),
-        lax.all_gather(up_bias, ("gx", "gy"), axis=0, tiled=True),
-        lax.all_gather(down_weight, ("gx", "gy"), axis=0, tiled=True),
-        lax.all_gather(down_bias, ("gx", "gy"), axis=0, tiled=True),
-    )
-    qkv_back = refetch[2]
-    out_back = refetch[4]
-    up_back = refetch[8]
-    down_back = refetch[10]
     upstream = rows_grad.astype(jnp.float32)
     grad_down_weight = trans_dot(active, rows_grad)
     grad_down_bias = jnp.sum(upstream, axis=0)
-    grad_active = back_dot(rows_grad, down_back)
+    grad_active = back_dot(rows_grad, down_full)
     grad_hidden = gelu_pull(grad_active)[0].astype(jnp.bfloat16)
     grad_up_weight = trans_dot(normed_two, grad_hidden)
     grad_up_bias = jnp.sum(grad_hidden.astype(jnp.float32), axis=0)
-    grad_normed_two = back_dot(grad_hidden, up_back)
+    grad_normed_two = back_dot(grad_hidden, up_full)
     grad_mid_norm, grad_gain_two, grad_shift_two = norm_two_pull(grad_normed_two)
     grad_middle = upstream + grad_mid_norm
     grad_branch = grad_middle.astype(jnp.bfloat16)
     grad_out_weight = trans_dot(context, grad_branch)
     grad_out_bias = jnp.sum(grad_branch.astype(jnp.float32), axis=0)
-    grad_context = back_dot(grad_branch, out_back).astype(jnp.bfloat16)
+    grad_context = back_dot(grad_branch, out_full).astype(jnp.bfloat16)
     grad_query_b, grad_key_b, grad_value_b = lax.map(
         attend_backward,
         (
@@ -295,42 +764,46 @@
             jnp.sum(grad_value.astype(jnp.float32), axis=0),
         ]
     )
-    grad_normed = back_dot(grad_joined, qkv_back)
+    grad_normed = back_dot(grad_joined, qkv_full)
     grad_in_norm, grad_gain_one, grad_shift_one = norm_one_pull(grad_normed)
     input_grads = (grad_middle + grad_in_norm).astype(jnp.bfloat16)
-    summed = (
-        lax.psum_scatter(grad_gain_one, ("gx", "gy"), scatter_dimension=0, tiled=True),
-        lax.psum_scatter(grad_shift_one, ("gx", "gy"), scatter_dimension=0, tiled=True),
-        lax.psum_scatter(grad_qkv_weight, ("gx", "gy"), scatter_dimension=0, tiled=True),
-        lax.psum_scatter(grad_qv_bias, ("gx", "gy"), scatter_dimension=1, tiled=True),
-        lax.psum_scatter(grad_out_weight, ("gx", "gy"), scatter_dimension=0, tiled=True),
-        lax.psum_scatter(grad_out_bias, ("gx", "gy"), scatter_dimension=0, tiled=True),
-        lax.psum_scatter(grad_gain_two, ("gx", "gy"), scatter_dimension=0, tiled=True),
-        lax.psum_scatter(grad_shift_two, ("gx", "gy"), scatter_dimension=0, tiled=True),
-        lax.psum_scatter(grad_up_weight, ("gx", "gy"), scatter_dimension=0, tiled=True),
-        lax.psum_scatter(grad_up_bias, ("gx", "gy"), scatter_dimension=0, tiled=True),
-        lax.psum_scatter(grad_down_weight, ("gx", "gy"), scatter_dimension=0, tiled=True),
-        lax.psum_scatter(grad_down_bias, ("gx", "gy"), scatter_dimension=0, tiled=True),
-    )
-    back_rows, back_grads = (
-        lax.all_to_all(
-            output_rows.reshape(gy_count, slot_capacity, model_width),
-            "gy",
-            split_axis=0,
-            concat_axis=0,
-            tiled=True,
-        ),
-        lax.all_to_all(
-            input_grads.reshape(gy_count, slot_capacity, model_width),
-            "gy",
-            split_axis=0,
-            concat_axis=0,
-            tiled=True,
-        ),
-    )
+
+    def terms(value):
+        return value.astype(jnp.bfloat16).reshape(chain, 2, 2, 2, -1, value.shape[-1])
+
+    vector_grads = [
+        grad_gain_one,
+        grad_shift_one,
+        grad_qv_bias[0],
+        grad_qv_bias[1],
+        grad_out_bias,
+        grad_gain_two,
+        grad_shift_two,
+        grad_down_bias,
+        grad_up_bias,
+    ]
+    vector_terms = jnp.stack(
+        [
+            jnp.pad(item.reshape(devices, -1), ((0, 0), (0, 128 - item.shape[0] // devices)))
+            for item in vector_grads
+        ],
+        axis=1,
+    )
+    vector_terms = jnp.pad(vector_terms, ((0, 0), (0, 16 - len(small)), (0, 0)))
+    sum_qkv, sum_out, sum_up, sum_down, sum_vectors = scatter_all(
+        chain,
+        [
+            terms(grad_qkv_weight),
+            terms(grad_out_weight),
+            terms(grad_up_weight),
+            terms(grad_down_weight),
+            vector_terms.reshape(chain, 2, 2, 2, 16, 128),
+        ],
+    )
+    sums = [sum_vectors[at, : item.shape[0]] for at, item in enumerate(small)]
     pick_rows = jnp.where(target < gy_count * slot_capacity, target, 0)
-    out_flat = back_rows.reshape(-1, model_width)[pick_rows]
-    grad_flat = back_grads.reshape(-1, model_width)[pick_rows]
+    out_flat = output_rows[pick_rows]
+    grad_flat = input_grads[pick_rows]
     zero_value = jnp.zeros((), jnp.bfloat16)
     out_tokens = jnp.where(visible[:, None], out_flat, zero_value).reshape(
         samples, patches, model_width
@@ -341,18 +814,18 @@
     return (
         out_tokens,
         grad_tokens,
-        summed[0],
-        summed[1],
-        summed[2],
-        summed[3],
-        summed[4],
-        summed[5],
-        summed[6],
-        summed[7],
-        summed[8],
-        summed[9],
-        summed[10],
-        summed[11],
+        sums[0],
+        sums[1],
+        sum_qkv,
+        jnp.stack([sums[2], sums[3]]),
+        sum_out,
+        sums[4],
+        sums[5],
+        sums[6],
+        sum_up,
+        sums[8],
+        sum_down,
+        sums[7],
     )
 
 

time: 827 us -> 513 us (0.62)
  waiting for transfers between devices: 356 us -> 0 us
  Pallas kernels: 0 us -> 196 us
  blocking collectives: 135 us -> 0 us
  local copies, waits for them, and re-layouts: 109 us -> 134 us
  starting transfers between devices: 16.5 us -> 0 us
  matrix products: 144 us -> 129 us
  between operations: 15.3 us -> 1.56 us
    reduce_scatter x4 -> x0, waiting for transfers between devices: 297 us -> none  [the longest x1 142 us: per_device(): lax.psum_scatter(grad_down_weight, ('gx', 'gy'), scatter_dimension=0, til...]
    pallas_call x0 -> x2, Pallas kernels: none -> 196 us  [the longest x1 128 us: scatter_all(): pl.pallas_call(functools.partial(scatter_kernel, chain, parts, count), ou...]
    unnamed x2 -> x0, blocking collectives: 95.9 us -> none
    all_gather x4 -> x0, waiting for transfers between devices: 52 us -> none  [the longest x1 52 us: per_device(): lax.all_gather(down_weight, ('gx', 'gy'), axis=0, tiled=True)]
    all_gather x1 -> x0, blocking collectives: 39.2 us -> none  [per_device(): lax.all_gather(qv_bias, ('gx', 'gy'), axis=1, tiled=True)]
    all_to_all x4 -> x0, starting transfers between devices: 16 us -> none  [the longest x1 4.28 us: per_device(): lax.all_to_all(send_grads.reshape(gy_count, slot_capacity, model_width),...]
    while x5 -> x4, local copies, waits for them, and re-layouts: 17.7 us -> 17.7 us  [per_device(): lax.map(attend_forward, (query_blocks, key_blocks, value_blocks, label_bl...]
  transfers between devices with their start and end apart: 12 -> 0, of which waited for: 5 -> 0; matrix products, arithmetic and copies ran while one was open for 30% -> 0% of each run, Pallas kernels for 0% -> 0%
where the time goes in v1:
time: 513 us; the launch traced here: 505 us
  Pallas kernels  196 us (38%)
  local copies, waits for them, and re-layouts  134 us (26%)
  matrix products  129 us (25%)
  other arithmetic  42.9 us (8%)
    pallas_call x1, Pallas kernels, scatter_all(): pl.pallas_call(functools.partial(scatter_kernel, chain, parts, count), ou...  128 us
    pallas_call x1, Pallas kernels, gather_all(): pl.pallas_call(functools.partial(gather_kernel, chain, parts, count), out...  68 us
    dot_general x4, matrix products, back_dot(): lax.dot_general(left, right, (((1,), (1,)), ((), ())), preferred_element_...  39.8 us
    dot_general x4, matrix products, trans_dot(): lax.dot_general(left, right, (((0,), (0,)), ((), ())), preferred_element_...  21 us
    while x4, local copies, waits for them, and re-layouts, per_device(): lax.map(attend_forward, (query_blocks, key_blocks, value_blocks, label_bl...  17.7 us
    unnamed x133, local copies, waits for them, and re-layouts  12.6 us
    convert_element_type x1, other arithmetic, per_device(): active = active_f.astype(jnp.bfloat16)  11 us

profile of v1, /device:TPU:0, one launch (start us, length us, event | category | flops | bytes accessed | tf_op | source)
XLA Modules:
  0.0 505.1 jit_solution(4263721773452895187)
XLA Ops:
  9.5 6.0 %scatter_custom_fusion.1 = bf16[768,768]{1,0:T(8,128)(2,1)S(1)} fusion(s32[1024]{0:T(1024)S(1)} %bitcast.232, bf16[1024,768]{1,0:T(8,128)(2,1)} %bitcast.238, bf16[]{:T(256)} %constant.83.clone.1), kind=kCustom, calls=%fused_computation.124 | custom fusion | bytes 1180160 | tf_op jit(solution)/shard_map/scatter | solution.py:680
  15.6 6.3 %scatter_custom_fusion = bf16[768,768]{1,0:T(8,128)(2,1)S(1)} fusion(s32[1024]{0:T(1024)S(1)} %bitcast.233, bf16[1024,768]{1,0:T(8,128)(2,1)} %bitcast.239, bf16[]{:T(256)} %constant.83.clone.1), kind=kCustom, calls=%fused_computation.126 | custom fusion | bytes 1180160 | tf_op jit(solution)/shard_map/scatter | solution.py:675
  23.2 1.5 copy.64
  24.6 68.0 %gather_all.1 = (bf16[32,24,2304]{2,1,0:T(8,128)(2,1)}, bf16[32,24,768]{2,1,0:T(8,128)(2,1)}, bf16[32,24,3072]{2,1,0:T(8,128)(2,1)}, bf16[32,96,768]{2,1,0:T(8,128)(2,1)}, bf16[32,16,128]{2,1,0:T(8,128)(2,1)}) custom-call(bf16[24,2304]{1,0:T(8,128)(2,1)} %refs_0_.1, bf16[24,768]{1,0:T(8,128)(2,1)} %refs_1_.1, bf16[24,3072]{1,0:T(8,128)(2,1)} %refs_2_.1, ...), custom_call_target="tpu_custom_call" | custom-call | tf_op jit(solution)/shard_map/gather_all/pallas_call | solution.py:295
  98.1 5.1 %fusion.76 = f32[768,2304]{1,0:T(8,128)S(1)} fusion(bf16[768,2304]{1,0:T(8,128)(2,1)} %bitcast.224, bf16[768,768]{0,1:T(8,128)(2,1)S(1)} %copy.54, f32[768]{0:T(1024)S(1)} %reshape.604, f32[768]{0:T(1024)S(1)} %reshape.603, f32[768]{0:T(1024)S(1)} %fusion.71, f32[768]{0:T(1024)S(1)} %broadcast_multiply_fusion.1), kind=kOutput, calls=%fused_computation.193 | convolution fusion | flops 2721447936 | bytes 11808768 | tf_op jit(solution)/shard_map/dot_general | solution.py:695
  105.8 3.2 reshape.644
  109.0 3.8 copy.59
  112.8 4.7 reshape.645
  117.5 4.8 copy.60
  122.3 4.7 reshape.643
  126.9 4.8 copy.58
  133.1 22.0 %while.26 = (s32[]{:T(128)}, bf16[4,1,192,12,64]{2,4,3,1,0:T(8,128)(2,1)}, f32[4,1,12,192]{3,2,1,0:T(8,128)}, bf16[4,1,192,12,64]{2,4,3,1,0:T(8,128)(2,1)}, s32[...) while((s32[]{:T(128)}, ...), condition=%wide.region_8.9_spmd, body=%wide.region_5.8_spmd.sunk | while | flops 118736640 | bytes 7126373 | solution.py:706
  133.7 1.6 fusion.125
  135.8 2.5 fusion.127
  139.1 1.6 fusion.125
  141.2 2.5 fusion.127
  144.4 1.6 fusion.125
  146.6 2.5 fusion.127
  149.8 1.6 fusion.125
  152.0 2.5 fusion.127
  155.1 4.3 copy.61
  159.4 4.0 reshape.582
  163.5 2.8 fusion.83
  167.8 6.4 %fusion.78 = f32[768,3072]{1,0:T(8,128)S(1)} fusion(bf16[768,3072]{1,0:T(8,128)(2,1)} %bitcast.219, f32[768,768]{0,1:T(8,128)S(1)} %get-tuple-element.245, f32[768]{0:T(1024)S(1)} %reshape.607, f32[768]{0:T(1024)S(1)} %reshape.606, f32[768]{0:T(1024)S(1)} %fusion.72, f32[768]{0:T(1024)S(1)} %broadcast_multiply_fusion), kind=kOutput, calls=%fused_computation.194 | convolution fusion | flops 3626827776 | bytes 16527360 | tf_op jit(solution)/shard_map/dot_general | solution.py:719
  174.3 27.4 %convert_reduce_fusion = (f32[3072]{0:T(1024)}, bf16[768,3072]{1,0:T(8,128)(2,1)S(1)}, f32[768,3072]{1,0:T(8,128)}) fusion(f32[768,3072]{1,0:T(8,128)S(1)} %fusion.78, f32[3072]{0:T(1024)S(1)} %copy-done.42, bf16[768,768]{1,0:T(8,128)(2,1)S(1)} %copy-done.15, bf16[3072,768]{1,0:T(8,128)(2,1)S(1)} %bitcast.237), kind=kOutput, calls=%fused_computation.67 | convolution fusion | flops 3800822784 | bytes 29515776 | tf_op jit(solution)/shard_map/dot_general | solution.py:560
  201.7 5.9 %fusion.85 = (f32[768]{0:T(1024)}, f32[768,768]{1,0:T(8,128)}) fusion(bf16[768,3072]{1,0:T(8,128)(2,1)S(1)} %get-tuple-element.214, bf16[768,3072]{1,0:T(8,128)(2,1)S(1)} %bitcast.222), kind=kOutput, calls=%fused_computation.199 | convolution fusion | flops 3624467712 | bytes 11799552 | tf_op jit(solution)/shard_map/dot_general | solution.py:560
  207.6 11.0 %multiply_convert_fusion.1 = bf16[768,3072]{1,0:T(8,128)(2,1)} fusion(f32[768,3072]{1,0:T(8,128)} %get-tuple-element.215, f32[768,3072]{1,0:T(8,128)} %copy-done.2, f32[3072]{0:T(1024)S(1)} %copy-done.43), kind=kLoop, calls=%fused_computation.69 | loop fusion | flops 9437184 | bytes 23605248 | tf_op jit(solution)/shard_map/convert_element_type | solution.py:723
  218.6 8.8 %add_convert_fusion.2 = bf16[768,768]{0,1:T(8,128)(2,1)} fusion(f32[768,768]{0,1:T(8,128)S(1)} %get-tuple-element.245, bf16[768,3072]{1,0:T(8,128)(2,1)} %multiply_convert_fusion.1, bf16[3072,768]{1,0:T(8,128)(2,1)} %bitcast.234, f32[768]{0:T(1024)S(1)} %copy-done.51), kind=kOutput, calls=%fused_computation.116 | convolution fusion | flops 3625648128 | bytes 12979200 | tf_op jit(solution)/shard_map/dot_general | solution.py:726
  227.4 5.6 %convolution_convert_fusion.3 = bf16[3072,768]{1,0:T(8,128)(2,1)} fusion(bf16[768,3072]{1,0:T(8,128)(2,1)S(1)} %copy-done.18, bf16[768,768]{1,0:T(8,128)(2,1)S(1)} %copy-done.15), kind=kOutput, calls=%fused_computation.84 | convolution fusion | flops 3626237952 | bytes 10616832 | tf_op jit(solution)/shard_map/dot_general | solution.py:554
  233.1 1.6 copy.63
  236.7 5.2 %gather_fusion = bf16[1024,768]{1,0:T(8,128)(2,1)} fusion(bf16[768,768]{1,0:T(8,128)(2,1)S(1)} %copy.63, s32[1024]{0:T(1024)S(1)} %copy-done.48), kind=kCustom, calls=%fused_computation | custom fusion | bytes 3149824 | tf_op jit(solution)/shard_map/gather | solution.py:805
  241.9 3.3 copy.65
  245.2 3.0 multiply_reduce_fusion.1
  248.2 8.3 %convolution_convert_fusion.4 = bf16[768,3072]{1,0:T(8,128)(2,1)} fusion(bf16[768,3072]{1,0:T(8,128)(2,1)} %copy-done.54, f32[768,768]{0,1:T(8,128)S(1)} %get-tuple-element.245, f32[768]{0:T(1024)S(1)} %copy-done.39, f32[768]{0:T(1024)S(1)} %copy-done.30, f32[768]{0:T(1024)S(1)} %copy-done.32, f32[768]{0:T(1024)S(1)} %copy-done.26), kind=kOutput, calls=%fused_computation.85 | convolution fusion | flops 3629187072 | bytes 11808768 | tf_op jit(solution)/shard_map/dot_general | solution.py:554
  256.6 2.0 fusion.81
  260.0 2.2 convert_reduce_fusion.5
  262.2 2.2 convolution_convert_fusion.5
  264.4 2.2 convolution_convert_fusion.6
  267.2 3.4 reshape.642
  270.6 3.2 copy.69
  277.8 36.8 %while.27 = (s32[]{:T(128)}, bf16[4,1,192,12,64]{2,4,3,1,0:T(8,128)(2,1)}, bf16[4,1,192,12,64]{2,4,3,1,0:T(8,128)(2,1)}, bf16[4,1,192,12,64]{2,4,3,1,0:T(8,128)(...) while((s32[]{:T(128)}, ...), condition=%wide.region_16.17_spmd, body=%wide.region_14.16_spmd.sunk | while | flops 287868672 | bytes 18529660 | solution.py:744
  279.3 1.6 fusion.136
  282.4 2.3 fusion.139
  288.5 1.6 fusion.136
  291.6 2.3 fusion.139
  297.7 1.6 fusion.136
  300.8 2.3 fusion.139
  306.9 1.6 fusion.136
  310.0 2.3 fusion.139
  314.7 2.8 copy.72
  317.4 2.6 reshape.589
  320.4 2.4 copy.73
  322.8 4.0 reshape.590
  329.1 2.2 reshape.588
  332.0 1.4 constant_dynamic-update-slice_fusion.2
  333.7 1.8 copy-done.19
  335.5 4.4 fusion.84
  339.9 4.9 convolution_convert_fusion.2
  345.4 2.2 copy.74
  348.3 1.6 fusion.59
  350.3 2.8 convert_reduce_fusion.4
  360.5 128.4 %scatter_all.1 = (f32[24,2304]{1,0:T(8,128)}, f32[24,768]{1,0:T(8,128)}, f32[24,3072]{1,0:T(8,128)}, f32[96,768]{1,0:T(8,128)}, f32[16,128]{1,0:T(8,128)}) custom-call(bf16[4,2,2,2,24,2304]{5,4,3,2,1,0:T(8,128)(2,1)} %bitcast.223, bf16[4,2,2,2,24,768]{5,4,3,2,1,0:T(8,128)(2,1)} %bitcast.226, bf16[4,2,2,2,24,3072]{5,4,3,2,1,0:T(8,128)(2,1)} %bitcast.218, ...), custom_call_target="tpu_custom_call" | custom-call | tf_op jit(solution)/shard_map/scatter_all/pallas_call | solution.py:524
  493.4 5.2 %gather_fusion.1 = bf16[1024,768]{1,0:T(8,128)(2,1)} fusion(bf16[768,768]{1,0:T(8,128)(2,1)S(1)} %copy.75, s32[1024]{0:T(1024)S(1)} %copy-done.49), kind=kCustom, calls=%fused_computation.1 | custom fusion | bytes 3149824 | tf_op jit(solution)/shard_map/gather | solution.py:806
  498.7 3.4 broadcast_select_fusion
  (249 shorter events, 75.0 us)
Async XLA Ops:
  15.6 7.6 %copy-start.14 = (bf16[768,768]{1,0:T(8,128)(2,1)}, bf16[768,768]{1,0:T(8,128)(2,1)S(1)}, u32[]{:S(2)}) copy-start(bf16[768,768]{1,0:T(8,128)(2,1)S(1)} %scatter_custom_fusion.1) | copy-start | bytes 3538948
  22.6 140.9 %copy-start = (bf16[768,768]{0,1:T(8,128)(2,1)}, bf16[768,768]{0,1:T(8,128)(2,1)S(1)}, u32[]{:S(2)}) copy-start(bf16[768,768]{0,1:T(8,128)(2,1)S(1)} %copy.54) | copy-start | bytes 3538948
  22.8 80.4 %copy-start.21 = (f32[768]{0:T(1024)}, f32[768]{0:T(1024)S(1)}, u32[]{:S(2)}) copy-start(f32[768]{0:T(1024)S(1)} %broadcast_multiply_fusion.1) | copy-start | bytes 9220
  23.2 74.6 %copy-start.44 = (f32[768]{0:T(1024)}, f32[768]{0:T(1024)S(1)}, u32[]{:S(2)}) copy-start(f32[768]{0:T(1024)S(1)} %fusion.60) | copy-start | bytes 9220
  23.2 80.1 %copy-start.27 = (f32[768]{0:T(1024)}, f32[768]{0:T(1024)S(1)}, u32[]{:S(2)}) copy-start(f32[768]{0:T(1024)S(1)} %fusion.71) | copy-start | bytes 9220
  97.7 5.5 %copy-start.23 = (f32[768]{0:T(1024)}, f32[768]{0:T(1024)S(1)}, u32[]{:S(2)}) copy-start(f32[768]{0:T(1024)S(1)} %reshape.603) | copy-start | bytes 9220
  97.8 69.4 %copy-start.29 = (f32[768]{0:T(1024)}, f32[768]{0:T(1024)S(1)}, u32[]{:S(2)}) copy-start(f32[768]{0:T(1024)S(1)} %reshape.606) | copy-start | bytes 9220
  97.9 69.3 %copy-start.38 = (f32[768]{0:T(1024)}, f32[768]{0:T(1024)S(1)}, u32[]{:S(2)}) copy-start(f32[768]{0:T(1024)S(1)} %reshape.607) | copy-start | bytes 9220
  98.0 5.3 %copy-start.36 = (f32[768]{0:T(1024)}, f32[768]{0:T(1024)S(1)}, u32[]{:S(2)}) copy-start(f32[768]{0:T(1024)S(1)} %reshape.604) | copy-start | bytes 9220
  155.1 4.4 copy-start.3
  155.1 8.4 %copy-start.41 = (s32[4,1,192]{2,1,0:T(1,128)}, s32[4,1,192]{2,1,0:T(1,128)S(1)}, u32[]{:S(2)}) copy-start(s32[4,1,192]{2,1,0:T(1,128)S(1)} %get-tuple-element.458) | copy-start | bytes 9220
  166.3 0.9 copy-start.25
  166.3 7.9 %slice-start.2 = ((s8[4718592]{0:T(1024)(128)(4,1)}), s8[4194304]{0:T(1024)(128)(4,1)S(1)}, s32[]{:S(2)}) async-start(s8[4718592]{0:T(1024)(128)(4,1)} %bitcast.235), calls=%async_computation.2 | async-start | bytes 8388608
  166.6 0.6 copy-start.46
  167.2 0.6 copy-start.31
  167.8 6.4 %copy-start.15 = (bf16[768,768]{1,0:T(8,128)(2,1)S(1)}, bf16[768,768]{1,0:T(8,128)(2,1)}, u32[]{:S(2)}) copy-start(bf16[768,768]{1,0:T(8,128)(2,1)} %copy-done.14) | copy-start | bytes 3538948
  167.8 6.4 %copy-start.42 = (f32[3072]{0:T(1024)S(1)}, f32[3072]{0:T(1024)}, u32[]{:S(2)}) copy-start(f32[3072]{0:T(1024)} %reshape.608) | copy-start | bytes 36868
  167.8 6.5 %slice-start.3 = ((s8[4718592]{0:T(1024)(128)(4,1)}), s8[524288]{0:T(1024)(128)(4,1)S(1)}, s32[]{:S(2)}) async-start(s8[4718592]{0:T(1024)(128)(4,1)} %bitcast.235), calls=%async_computation.3 | async-start | bytes 1048576
  167.8 33.9 %slice-start = ((s8[4718592]{0:T(1024)(128)(4,1)}), s8[4194304]{0:T(1024)(128)(4,1)S(1)}, s32[]{:S(2)}) async-start(s8[4718592]{0:T(1024)(128)(4,1)} %bitcast.220), calls=%async_computation | async-start | bytes 8388608
  174.3 27.4 %copy-start.2 = (f32[768,3072]{1,0:T(8,128)}, f32[768,3072]{1,0:T(8,128)S(1)}, u32[]{:S(2)}) copy-start(f32[768,3072]{1,0:T(8,128)S(1)} %fusion.78) | copy-start | bytes 28311556
  174.3 27.4 %slice-start.1 = ((s8[4718592]{0:T(1024)(128)(4,1)}), s8[524288]{0:T(1024)(128)(4,1)S(1)}, s32[]{:S(2)}) async-start(s8[4718592]{0:T(1024)(128)(4,1)} %bitcast.220), calls=%async_computation.1 | async-start | bytes 1048576
  201.6 5.9 %copy-start.54 = (bf16[768,3072]{1,0:T(8,128)(2,1)}, bf16[768,3072]{1,0:T(8,128)(2,1)S(1)}, u32[]{:S(2)}) copy-start(bf16[768,3072]{1,0:T(8,128)(2,1)S(1)} %get-tuple-element.214) | copy-start | bytes 14155780
  201.7 5.9 %copy-start.43 = (f32[3072]{0:T(1024)S(1)}, f32[3072]{0:T(1024)}, u32[]{:S(2)}) copy-start(f32[3072]{0:T(1024)} %reshape.608) | copy-start | bytes 36868
  207.6 11.0 %copy-start.51 = (f32[768]{0:T(1024)S(1)}, f32[768]{0:T(1024)}, u32[]{:S(2)}) copy-start(f32[768]{0:T(1024)} %reshape.609) | copy-start | bytes 9220
  218.6 8.8 %copy-start.18 = (bf16[768,3072]{1,0:T(8,128)(2,1)S(1)}, bf16[768,3072]{1,0:T(8,128)(2,1)}, u32[]{:S(2)}) copy-start(bf16[768,3072]{1,0:T(8,128)(2,1)} %multiply_convert_fusion.1) | copy-start | bytes 14155780
  233.1 1.6 copy-start.50
  233.1 3.6 copy-start.48
  241.9 3.3 copy-start.26
  241.9 3.3 copy-start.30
  241.9 3.3 copy-start.32
  245.2 3.0 copy-start.39
  248.2 8.3 %copy-start.47 = (f32[768]{0:T(1024)S(1)}, f32[768]{0:T(1024)}, u32[]{:S(2)}) copy-start(f32[768]{0:T(1024)} %copy-done.46) | copy-start | bytes 9220
  248.2 8.3 %copy-start.6 = (f32[768,768]{0,1:T(8,128)S(1)}, f32[768,768]{0,1:T(8,128)}, u32[]{:S(2)}) copy-start(f32[768,768]{0,1:T(8,128)} %copy.65) | copy-start | bytes 7077892
  256.6 3.4 copy-start.10
  260.0 2.2 copy-start.20
  262.2 2.2 copy-start.53
  273.8 4.1 copy-start.4
  273.8 4.1 copy-start.5
  314.7 5.4 %copy-start.8 = (bf16[4,1,192,12,64]{2,4,3,1,0:T(8,128)(2,1)S(1)}, bf16[4,1,192,12,64]{2,4,3,1,0:T(8,128)(2,1)}, u32[]{:S(2)}) copy-start(bf16[4,1,192,12,64]{2,4,3,1,0:T(8,128)(2,1)} %get-tuple-element.125) | copy-start | bytes 3538948
  320.4 7.1 %copy-start.9 = (bf16[4,1,192,12,64]{2,4,3,1,0:T(8,128)(2,1)S(1)}, bf16[4,1,192,12,64]{2,4,3,1,0:T(8,128)(2,1)}, u32[]{:S(2)}) copy-start(bf16[4,1,192,12,64]{2,4,3,1,0:T(8,128)(2,1)} %get-tuple-element.123) | copy-start | bytes 3538948
  329.0 4.4 copy-start.16
  332.0 1.6 copy-start.17
  333.4 2.0 copy-start.19
  335.5 4.4 copy-start.1
  335.5 4.4 copy-start.22
  335.5 4.4 copy-start.24
  335.5 4.4 copy-start.28
  335.5 4.4 copy-start.37
  347.6 0.7 copy-start.45
  348.3 1.7 copy-start.7
  348.3 2.0 copy-start.11
  360.5 132.2 %copy-start.13 = (bf16[768,768]{0,1:T(8,128)(2,1)S(1)}, bf16[768,768]{0,1:T(8,128)(2,1)}, u32[]{:S(2)}) copy-start(bf16[768,768]{0,1:T(8,128)(2,1)} %get-tuple-element.229) | copy-start | bytes 3538948
  488.9 4.5 copy-start.49
  493.4 5.2 %copy-start.12 = (bf16[1024,768]{1,0:T(8,128)(2,1)S(1)}, bf16[1024,768]{1,0:T(8,128)(2,1)}, u32[]{:S(2)}) copy-start(bf16[1024,768]{1,0:T(8,128)(2,1)} %gather_fusion) | copy-start | bytes 4718596
  493.4 5.2 %copy-start.52 = (pred[8,128]{1,0:T(8,128)(4,1)S(1)}, pred[8,128]{1,0:T(8,128)(4,1)}, u32[]{:S(2)}) copy-start(pred[8,128]{1,0:T(8,128)(4,1)} %get-tuple-element.221) | copy-start | bytes 3076
  498.7 3.5 copy-start.35
  498.7 4.2 copy-start.40
  498.7 4.8 copy-start.34
  498.7 5.5 %copy-start.33 = (f32[96,768]{1,0:T(8,128)S(1)}, f32[96,768]{1,0:T(8,128)}, u32[]{:S(2)}) copy-start(f32[96,768]{1,0:T(8,128)} %get-tuple-element.453) | copy-start | bytes 884740
